TPU v7x, 512 devices: a whole 4x4x16 slice. The times are simulated.
512 devices in a mesh: row: 32 (over z, core), col: 16 (over y, x).
Axes of the slice: x: 4, y: 4, z: 16, core: 2. Of those that a mesh axis runs over, the one named last changes fastest.
Arguments:
- coeffs: bfloat16 [4096, 64, 128], P(('row', 'col')), may hold values from -6 to 6
- blocks: bfloat16 [262144, 64, 64], P(('row', 'col')), may hold values from -0.046875 to 0.046875
- blk_rows: int32 [262144], P(('row', 'col')), may hold values from 0 to 4095, as said below
- blk_cols: int32 [262144], P(('row', 'col')), may hold values from 0 to 4095, as said below
- blk_count: int32 [512], P(('row', 'col')), may hold values from 0 to 512, as said below
Outputs:
- product: float32 [4096, 64, 128], P(('row', 'col'))
Inputs may be any that keep to these rules, and one draw needn't show every extreme that they name: `blk_rows`: element e belongs to device e // 8 in row+col order. In the first blk_count slots of a device, I <= J, I belongs to a device of the same row index, and J to a device of the same column index whose row index exceeds that of I's device by 0 to 3; the difference 3 occurs in every draw. Later slots hold elements of the device's own row and column groups and are unused; pairs may repeat. `blk_cols`: see blk_rows. `blk_count`: counts differ widely between devices; some device uses all 512 slots in every draw.
All inputs are finite; a program needn't handle non-finite values.
Results may differ from a plain program's by a relative error of at most 0.0003.
Values may be sent and summed in bfloat16 or wider, within the bound.
A program may use at most 128 MiB of HBM per device.

v0:
```python
import jax
import jax.numpy as jnp
from jax import lax
from jax.sharding import PartitionSpec as P

REACH = 3


def from_behind(block, axis, distance):
    devices = range(lax.axis_size(axis))
    route = [(i - distance, i) for i in devices if i - distance in devices]
    return lax.ppermute(block, axis, route)


def body(coeffs, blocks, blk_rows, blk_cols, blk_count):
    high_precision = lax.Precision.HIGHEST
    elem_dev, width, sides = coeffs.shape
    slot_total = blocks.shape[0]
    my_row = lax.axis_index("row")
    segment = elem_dev * lax.axis_size("col")
    window = (REACH + 1) * elem_dev
    row_group = lax.all_gather(coeffs, "col", axis=0, tiled=True)
    pieces = [coeffs]
    for offset in range(1, REACH + 1):
        pieces.append(from_behind(coeffs, "row", -offset))
    nearby = jnp.concatenate(pieces, axis=0)
    active = jnp.arange(slot_total, dtype=jnp.int32) < blk_count[0]
    mirror = active & (blk_rows != blk_cols)
    row_local = jnp.clip(blk_rows - my_row * segment, 0, segment - 1)
    col_local = (blk_cols // segment - my_row) * elem_dev + blk_cols % elem_dev
    col_local = jnp.clip(col_local, 0, window - 1)
    column_entries = nearby[col_local]
    row_contributions = jnp.einsum(
        "gjc,gcx->gjx", blocks, column_entries, preferred_element_type=jnp.float32
    )
    row_contributions = row_contributions.reshape(slot_total, width * sides)
    row_select = (
        (row_local[None, :] == jnp.arange(segment, dtype=jnp.int32)[:, None]) & active[None, :]
    ).astype(jnp.float32)
    row_entries = row_group[row_local]
    column_contributions = jnp.einsum(
        "ihv,ihe->ive", blocks, row_entries, preferred_element_type=jnp.float32
    )
    column_contributions = column_contributions.reshape(slot_total, width * sides)
    col_select = (
        (col_local[None, :] == jnp.arange(window, dtype=jnp.int32)[:, None]) & mirror[None, :]
    ).astype(jnp.float32)
    col_part = jnp.dot(
        col_select,
        column_contributions,
        precision=high_precision,
        preferred_element_type=jnp.float32,
    )
    row_part = jnp.dot(
        row_select, row_contributions, precision=high_precision, preferred_element_type=jnp.float32
    )
    row_sums = lax.psum_scatter(row_part, "col", scatter_dimension=0, tiled=True)
    col_sums = col_part[:elem_dev]
    for offset in range(1, REACH + 1):
        piece = col_part[offset * elem_dev : (offset + 1) * elem_dev]
        col_sums = col_sums + from_behind(piece, "row", offset)
    return (row_sums + col_sums).reshape(elem_dev, width, sides)


def solution(mesh):
    placed = (
        P(("row", "col"), None, None),
        P(("row", "col"), None, None),
        P(("row", "col")),
        P(("row", "col")),
        P(("row", "col")),
    )
    return jax.shard_map(
        body, mesh=mesh, in_specs=placed, out_specs=P(("row", "col"), None, None), check_vma=False
    )
```

profile of v0, /device:TPU:1, one launch (start us, length us, event | category | flops | bytes accessed | tf_op | source)
XLA Modules:
  0.0 232.6 jit_solution(14114727317031092291)
XLA Ops:
  6.5 0.0 copy-start
  6.5 0.0 all-gather.2.cloned.1.call-start
  6.5 0.7 all-gather.2.cloned.1.call-update
  7.3 0.0 all-reduce.3.cloned.1.call-start
  7.3 8.8 %collective-permute-start = (bf16[8,64,128]{2,1,0:T(8,128)(2,1)}, bf16[8,64,128]{2,1,0:T(8,128)(2,1)S(1)}, u32[]{:S(2)}, u32[]{:S(2)}) collective-permute-start(bf16[8,64,128]{2,1,0:T(8,128)(2,1)} %param.5), channel_id=1, source_target_pairs={{16,0},{32,16},{48,32},{64,48},{80,64},{96,80},{112,96},{128,112},... | collective-permute-start | bytes 393224 | tf_op jit(solution)/shard_map/ppermute | solution.py:12
  16.1 1.3 collective-permute-start.1
  17.4 1.3 collective-permute-start.2
  19.3 0.7 compare_select_fusion.1
  20.0 0.7 compare_select_fusion
  20.7 15.7 %copy.10 = bf16[512,64,64]{1,2,0:T(8,128)(2,1)} copy(bf16[512,64,64]{0,2,1:T(8,128)(2,1)} %param.6) | data formatting | bytes 8388608 | tf_op args[1]
  36.4 0.0 collective-permute-done
  36.4 0.0 collective-permute-done.1
  36.4 0.0 collective-permute-done.2
  36.4 0.0 copy-done
  36.4 0.1 pad_maximum_fusion
  36.5 13.4 %gather_fusion = bf16[512,64,128]{2,1,0:T(8,128)(2,1)} fusion(bf16[32,64,128]{2,1,0:T(8,128)(2,1)S(1)} %pad_maximum_fusion, s32[1024]{0:T(1024)S(1)} %pad_clamp_fusion.1), kind=kCustom, calls=%fused_computation | custom fusion | bytes 16779264 | tf_op jit(solution)/shard_map/gather | solution.py:32
  49.9 14.4 %fusion.27 = f32[512,128,64]{1,2,0:T(8,128)} fusion(bf16[512,64,64]{1,2,0:T(8,128)(2,1)} %copy.10, bf16[512,64,128]{2,1,0:T(8,128)(2,1)} %gather_fusion), kind=kOutput, calls=%fused_computation.44 | convolution fusion | flops 536870912 | bytes 29360128 | tf_op jit(solution)/shard_map/gjc,gcx->gjx/dot_general | solution.py:33
  64.3 0.0 copy-start.1
  64.3 0.0 copy-start.2
  64.3 24.6 %fusion.3 = f32[128,8192]{1,0:T(8,128)} fusion(f32[64,8,64,128]{3,2,1,0:T(8,128)} %bitcast.21, s32[512]{0:T(512)S(1)} %get-tuple-element.8, pred[512]{0:T(512)(128)(4,1)S(1)} %iota_compare_fusion.2), kind=kOutput, calls=%fused_computation.5 | convolution fusion | flops 6442582016 | bytes 20974080 | tf_op jit(solution)/shard_map/dot_general | solution.py:54
  88.9 0.0 all-reduce.3.cloned.1.call-update
  89.0 0.0 copy-done.1
  89.0 0.0 copy-done.2
  89.0 0.0 all-gather.2.cloned.1.call-done
  89.0 21.2 %gather_fusion.1 = bf16[512,64,128]{2,1,0:T(8,128)(2,1)} fusion(bf16[128,64,128]{2,1,0:T(8,128)(2,1)} %all-gather.2.cloned.1.call-done, s32[1024]{0:T(1024)S(1)} %pad_clamp_fusion), kind=kCustom, calls=%fused_computation.1 | custom fusion | bytes 16779264 | tf_op jit(solution)/shard_map/gather | solution.py:40
  110.3 14.2 %fusion.28 = f32[512,128,64]{1,2,0:T(8,128)} fusion(bf16[512,64,64]{1,2,0:T(8,128)(2,1)} %copy.10, bf16[512,64,128]{2,1,0:T(8,128)(2,1)} %gather_fusion.1), kind=kOutput, calls=%fused_computation.45 | convolution fusion | flops 536870912 | bytes 29360128 | tf_op jit(solution)/shard_map/ihv,ihe->ive/dot_general | solution.py:41
  124.5 20.5 %fusion = f32[32,8192]{1,0:T(8,128)S(1)} fusion(f32[64,8,64,128]{3,2,1,0:T(8,128)} %bitcast.20, s32[512]{0:T(512)S(1)} %get-tuple-element.6, pred[512]{0:T(512)(128)(4,1)S(1)} %compare_and_fusion), kind=kOutput, calls=%fused_computation.2 | convolution fusion | flops 1610645504 | bytes 17828352 | tf_op jit(solution)/shard_map/dot_general | solution.py:48
  145.0 0.1 fusion.26
  145.1 3.6 %collective-permute-start.3 = (f32[8,8192]{1,0:T(8,128)S(1)}, f32[8,8192]{1,0:T(8,128)S(1)}, u32[]{:S(2)}, u32[]{:S(2)}) collective-permute-start(f32[8,8192]{1,0:T(8,128)S(1)} %get-tuple-element.9), channel_id=1, source_target_pairs={{0,16},{16,32},{32,48},{48,64},{64,80},{80,96},{96,112},{112,128},... | collective-permute-start | bytes 786440 | tf_op jit(solution)/shard_map/ppermute | solution.py:12
  148.7 3.8 %collective-permute-start.4 = (f32[8,8192]{1,0:T(8,128)S(1)}, f32[8,8192]{1,0:T(8,128)S(1)}, u32[]{:S(2)}, u32[]{:S(2)}) collective-permute-start(f32[8,8192]{1,0:T(8,128)S(1)} %get-tuple-element.11), channel_id=1, source_target_pairs={{0,32},{16,48},{32,64},{48,80},{64,96},{80,112},{96,128},{112,144}... | collective-permute-start | bytes 786440 | tf_op jit(solution)/shard_map/ppermute | solution.py:12
  152.5 4.0 %collective-permute-start.5 = (f32[8,8192]{1,0:T(8,128)S(1)}, f32[8,8192]{1,0:T(8,128)S(1)}, u32[]{:S(2)}, u32[]{:S(2)}) collective-permute-start(f32[8,8192]{1,0:T(8,128)S(1)} %get-tuple-element.10), channel_id=1, source_target_pairs={{0,48},{16,64},{32,80},{48,96},{64,112},{80,128},{96,144},{112,160... | collective-permute-start | bytes 786440 | tf_op jit(solution)/shard_map/ppermute | solution.py:12
  156.5 1.3 dynamic-slice
  158.4 0.0 collective-permute-done.3
  158.4 0.0 collective-permute-done.4
  158.5 5.6 %collective-permute-done.5 = f32[8,8192]{1,0:T(8,128)S(1)} collective-permute-done((f32[8,8192]{1,0:T(8,128)S(1)}, f32[8,8192]{1,0:T(8,128)S(1)}, u32[]{:S(2)}, u32[]{:S(2)}) %collective-permute-start.5) | collective-permute-done | bytes 262176 | tf_op jit(solution)/shard_map/ppermute | solution.py:12
  164.0 59.9 %all-reduce.3.cloned.1.call-done = f32[128,8192]{1,0:T(8,128)} async-done(((f32[128,8192]{1,0:T(8,128)}), f32[128,8192]{1,0:T(8,128)}) %all-reduce.3.cloned.1.call-update) | async-done | bytes 4194320
  224.0 1.0 fusion.9
  225.0 0.8 copy.11
  (4 shorter events, 0.0 us)
Async XLA Ops:
  6.5 29.9 %copy-start = (bf16[8,64,128]{2,1,0:T(8,128)(2,1)S(1)}, bf16[8,64,128]{2,1,0:T(8,128)(2,1)}, u32[]{:S(2)}) copy-start(bf16[8,64,128]{2,1,0:T(8,128)(2,1)} %param.5) | copy-start | bytes 393220
  6.5 82.5 %all-gather.2.cloned.1.call-start = ((), (), s32[]{:S(2)}) async-start(), calls=%async_computation | async-start | bytes 2228224 | tf_op jit(solution)/shard_map/all_gather | solution.py:22
  7.3 216.7 %all-reduce.3.cloned.1.call-start = ((), (), s32[]{:S(2)}) async-start(), calls=%async_computation.1 | async-start | bytes 8388608
  7.3 29.1 %collective-permute-start = (bf16[8,64,128]{2,1,0:T(8,128)(2,1)}, bf16[8,64,128]{2,1,0:T(8,128)(2,1)S(1)}, u32[]{:S(2)}, u32[]{:S(2)}) collective-permute-start(bf16[8,64,128]{2,1,0:T(8,128)(2,1)} %param.5), channel_id=1, source_target_pairs={{16,0},{32,16},{48,32},{64,48},{80,64},{96,80},{112,96},{128,112},... | collective-permute-start | bytes 393224 | tf_op jit(solution)/shard_map/ppermute | solution.py:12
  16.1 20.3 %collective-permute-start.1 = (bf16[8,64,128]{2,1,0:T(8,128)(2,1)}, bf16[8,64,128]{2,1,0:T(8,128)(2,1)S(1)}, u32[]{:S(2)}, u32[]{:S(2)}) collective-permute-start(bf16[8,64,128]{2,1,0:T(8,128)(2,1)} %param.5), channel_id=1, source_target_pairs={{32,0},{48,16},{64,32},{80,48},{96,64},{112,80},{128,96},{144,112}... | collective-permute-start | bytes 393224 | tf_op jit(solution)/shard_map/ppermute | solution.py:12
  17.4 19.0 %collective-permute-start.2 = (bf16[8,64,128]{2,1,0:T(8,128)(2,1)}, bf16[8,64,128]{2,1,0:T(8,128)(2,1)S(1)}, u32[]{:S(2)}, u32[]{:S(2)}) collective-permute-start(bf16[8,64,128]{2,1,0:T(8,128)(2,1)} %param.5), channel_id=1, source_target_pairs={{48,0},{64,16},{80,32},{96,48},{112,64},{128,80},{144,96},{160,112... | collective-permute-start | bytes 393224 | tf_op jit(solution)/shard_map/ppermute | solution.py:12
  64.3 24.6 %copy-start.1 = (s32[512]{0:T(512)S(1)}, s32[512]{0:T(512)}, u32[]{:S(2)}) copy-start(s32[512]{0:T(512)} %param.7) | copy-start | bytes 6148
  64.3 24.7 %copy-start.2 = (s32[512]{0:T(512)S(1)}, s32[512]{0:T(512)}, u32[]{:S(2)}) copy-start(s32[512]{0:T(512)} %param.8) | copy-start | bytes 6148
  145.1 13.4 %collective-permute-start.3 = (f32[8,8192]{1,0:T(8,128)S(1)}, f32[8,8192]{1,0:T(8,128)S(1)}, u32[]{:S(2)}, u32[]{:S(2)}) collective-permute-start(f32[8,8192]{1,0:T(8,128)S(1)} %get-tuple-element.9), channel_id=1, source_target_pairs={{0,16},{16,32},{32,48},{48,64},{64,80},{80,96},{96,112},{112,128},... | collective-permute-start | bytes 786440 | tf_op jit(solution)/shard_map/ppermute | solution.py:12
  148.7 9.8 %collective-permute-start.4 = (f32[8,8192]{1,0:T(8,128)S(1)}, f32[8,8192]{1,0:T(8,128)S(1)}, u32[]{:S(2)}, u32[]{:S(2)}) collective-permute-start(f32[8,8192]{1,0:T(8,128)S(1)} %get-tuple-element.11), channel_id=1, source_target_pairs={{0,32},{16,48},{32,64},{48,80},{64,96},{80,112},{96,128},{112,144}... | collective-permute-start | bytes 786440 | tf_op jit(solution)/shard_map/ppermute | solution.py:12
  152.5 11.5 %collective-permute-start.5 = (f32[8,8192]{1,0:T(8,128)S(1)}, f32[8,8192]{1,0:T(8,128)S(1)}, u32[]{:S(2)}, u32[]{:S(2)}) collective-permute-start(f32[8,8192]{1,0:T(8,128)S(1)} %get-tuple-element.10), channel_id=1, source_target_pairs={{0,48},{16,64},{32,80},{48,96},{64,112},{80,128},{96,144},{112,160... | collective-permute-start | bytes 786440 | tf_op jit(solution)/shard_map/ppermute | solution.py:12
Sparse Core Ops, SparseCore 0:
  10.4 64.7 all-gather.1
  89.1 134.8 all-reduce.2
where the time goes:
time: 233 us
  matrix products  73.7 us (32%)
  waiting for transfers between devices  66.3 us (28%)
  local copies, waits for them, and re-layouts  52.4 us (22%)
  starting transfers between devices  22.8 us (10%)
  between operations  14.9 us (6%)
  other arithmetic  2.49 us (1%)
    unnamed x3, waiting for transfers between devices  60.7 us
    dot_general x1, matrix products, body(): jnp.dot(row_select, row_contributions, precision=high_precision, preferre...  24.6 us
    ppermute x6, starting transfers between devices, from_behind(): return lax.ppermute(block, axis, route)  22.8 us
    gather x1, local copies, waits for them, and re-layouts, body(): row_entries = row_group[row_local]  21.2 us
    dot_general x1, matrix products, body(): jnp.dot(col_select, column_contributions, precision=high_precision, prefe...  20.5 us
    unnamed x8, local copies, waits for them, and re-layouts  16.9 us
    dot_general x1, matrix products, body(): jnp.einsum('gjc,gcx->gjx', blocks, column_entries, preferred_element_type...  14.4 us
    dot_general x1, matrix products, body(): jnp.einsum('ihv,ihe->ive', blocks, row_entries, preferred_element_type=jn...  14.2 us
  transfers between devices with their start and end apart: 8, of which 2 were waited for; matrix products, arithmetic and copies ran while one was open for 55% of the time, Pallas kernels for 0%

commit v1 on v0

v1 whole, which is shorter than its diff:
```python
import jax
import jax.numpy as jnp
from jax import lax
from jax.experimental import pallas as pl
from jax.experimental.pallas import tpu as pltpu
from jax.sharding import PartitionSpec as P

MESH = pl.DeviceIdType.MESH
F32, BF16, I16, I32 = jnp.float32, jnp.bfloat16, jnp.int16, jnp.int32

K = 64
NRHS = 128
ELEM = 8
SLOTS = 512
HALF = SLOTS // 2
REACH = 3
SIDE = 4
COLS = SIDE * SIDE
GROUP = ELEM * COLS
WINDOW = ELEM * (REACH + 1)
QUART = ELEM // 2
UNROLL = 16
STEP = 32767.0

T_COL, T_ROW = 0, SLOTS
T_PREV_ROW, T_PREV_COL = 2 * SLOTS, 3 * SLOTS
T_LAST_ROW = 4 * SLOTS
T_LAST_COL = T_LAST_ROW + 2 * GROUP


def nn(a, b):
    return lax.dot_general(a, b, (((1,), (0,)), ((), ())), preferred_element_type=F32)


def nt(a, b):
    return lax.dot_general(a, b, (((1,), (1,)), ((), ())), preferred_element_type=F32)


def add_terms(terms, table, prev, hist):
    for p, one, two in terms:
        hist[p] = one + hist[table[prev + p]]
        hist[p + HALF] = two + hist[table[prev + HALF + p]]


def row_terms(i, table, near, mats, hist):
    zero = jnp.zeros((K, NRHS), BF16)
    terms = []
    for u in range(UNROLL):
        p = i * UNROLL + u
        one, two = near[table[T_COL + p]], near[table[T_COL + HALF + p]]
        pair = mats[pl.ds(pl.multiple_of(p * K, K), K), :].astype(BF16)
        both = jnp.concatenate(
            [jnp.concatenate([one, zero], 1), jnp.concatenate([zero, two], 1)], 0
        )
        t = nn(pair, both)
        terms.append((p, t[:, :NRHS], t[:, NRHS:]))
    add_terms(terms, table, T_PREV_ROW, hist)


def col_terms(i, table, group, mats, hist):
    terms = []
    for u in range(UNROLL):
        p = i * UNROLL + u
        one, two = group[table[T_ROW + p]], group[table[T_ROW + HALF + p]]
        pair = mats[pl.ds(pl.multiple_of(p * K, K), K), :].T.astype(BF16)
        terms.append((p, nn(pair[:K], one), nn(pair[K:], two)))
    add_terms(terms, table, T_PREV_COL, hist)


def total(table, first, size, e, hist):
    return hist[table[first + e]] + hist[table[first + size + e]]


def coded(value):
    peak = jnp.max(jnp.abs(value), axis=0, keepdims=True)
    safe = jnp.maximum(peak, 1e-30)
    codes = jnp.round(value * (STEP / safe)).astype(I32).astype(I16)
    return codes, safe * (1.0 / STEP)


def decoded(codes, step):
    return codes.astype(I32).astype(F32) * step


def kernel(
    table, coeffs, blocks, out,
    flat, mats, hist, group, near, own, mine,
    send1, step1, got1, gstep1, send2, step2, got2, gstep2,
    sendc, stepc, gotc, gstepc,
    load_sem, ag_send, ag_recv, win_send, win_recv, s1_send, s1_recv, s2_send, s2_recv, c_send, c_recv,
):
    row, col = lax.axis_index("row"), lax.axis_index("col")
    n_row = lax.axis_size("row")
    at = (lax.rem(col, SIDE), lax.div(col, SIDE))

    def place(k, a, b):
        return b * SIDE + a if k == 0 else a * SIDE + b

    def shift(v, by):
        return lax.rem(v + by + SIDE, SIDE)

    def send(src, dst, s, r, device):
        return pltpu.make_async_remote_copy(
            src_ref=src, dst_ref=dst, send_sem=s, recv_sem=r, device_id=device, device_id_type=MESH
        )

    chunk = K * K // 4
    loads = [
        pltpu.make_async_copy(
            blocks.at[pl.ds(i * chunk, chunk)], flat.at[pl.ds(i * chunk, chunk)], load_sem.at[i]
        )
        for i in range(4)
    ]
    for c in loads:
        c.start()
    group[pl.ds(pl.multiple_of(col * ELEM, ELEM), ELEM)] = coeffs[...]
    near[pl.ds(0, ELEM)] = coeffs[...]
    near[pl.ds(ELEM, WINDOW - ELEM)] = jnp.zeros((WINDOW - ELEM, K, NRHS), BF16)
    gotc[...] = jnp.zeros_like(gotc)
    gstepc[...] = jnp.zeros_like(gstepc)

    barrier = pltpu.get_barrier_semaphore()
    for k in range(2):
        for by in range(1, SIDE):
            peer = place(k, shift(at[k], by), at[1 - k])
            pl.semaphore_signal(barrier, inc=1, device_id={"col": peer}, device_id_type=MESH)
    count = 2 * (SIDE - 1)
    for o in range(1, REACH + 1):
        for r in (row - o, row + o):
            inside = (r >= 0) & (r < n_row)

            @pl.when(inside)
            def _(r=r):
                pl.semaphore_signal(barrier, inc=1, device_id={"row": r}, device_id_type=MESH)

            count = count + jnp.where(inside, 1, 0)
    pl.semaphore_wait(barrier, count)

    def window(o, peer):
        return send(
            coeffs, near.at[pl.ds(o * ELEM, ELEM)], win_send.at[o - 1], win_recv.at[o - 1], {"row": peer}
        )

    for o in range(1, REACH + 1):

        @pl.when(row - o >= 0)
        def _(o=o):
            window(o, row - o).start()

    def piece(k, da, db, part=None):
        dev = place(k, shift(at[k], da), shift(at[1 - k], db))
        if part is None:
            return group.at[pl.ds(dev * ELEM + k * QUART, QUART)]
        return group.at[pl.ds(dev * ELEM + k * QUART + part * (QUART // 2), QUART // 2)]

    started = []

    def gather(k, axis, da, db, part, to, index):
        a, b = (shift(at[k], to), at[1 - k]) if axis == 0 else (at[k], shift(at[1 - k], to))
        ref = piece(k, da, db, part)
        c = send(ref, ref, ag_send.at[k, index], ag_recv.at[k, index], {"col": place(k, a, b)})
        c.start()
        started.append(c)

    def arrived(k, da, db, part, index):
        ref = piece(k, da, db, part)
        send(ref, ref, ag_send.at[k, index], ag_recv.at[k, index], {"col": col}).wait_recv()

    def along(k, da):
        q = (0, 2, 3, 1)[da + 0] if da >= 0 else 1
        gather(k, 1, da, 0, None, 1, 4 + 4 * q)
        gather(k, 1, da, 0, None, -1, 5 + 4 * q)

    def across(k, da):
        q = (0, 2, 3, 1)[da + 0] if da >= 0 else 1
        arrived(k, da, -1, None, 4 + 4 * q)
        gather(k, 1, da, -1, 0, 1, 6 + 4 * q)
        arrived(k, da, 1, None, 5 + 4 * q)
        gather(k, 1, da, 1, 1, -1, 7 + 4 * q)

    def last(k, da):
        q = (0, 2, 3, 1)[da + 0] if da >= 0 else 1
        arrived(k, da, 2, 0, 6 + 4 * q)
        arrived(k, da, 2, 1, 7 + 4 * q)

    for k in range(2):
        gather(k, 0, 0, 0, None, 1, 0)
        gather(k, 0, 0, 0, None, -1, 1)
    for k in range(2):
        along(k, 0)

    r = lax.broadcasted_iota(I32, (HALF, HALF), 0)
    c = lax.broadcasted_iota(I32, (HALF, HALF), 1)
    eye = jnp.where(r == c, 1.0, 0.0).astype(BF16)

    def turn(i, _):
        for u in range(8):
            j = i * 8 + u
            a = flat[pl.ds(pl.multiple_of(j * K, K), K), :]
            a = jnp.concatenate([a[:, :HALF], a[:, HALF:]], axis=0)
            mats[pl.ds(j, HALF, stride=K), :] = nt(eye, a)
        return 0

    loads[0].wait()
    loads[1].wait()
    lax.fori_loop(0, 4, turn, 0)
    for k in range(2):
        arrived(k, -1, 0, None, 0)
        gather(k, 0, -1, 0, 0, 1, 2)
        arrived(k, 1, 0, None, 1)
        gather(k, 0, 1, 0, 1, -1, 3)
        along(k, -1)
        along(k, 1)
    loads[2].wait()
    loads[3].wait()
    lax.fori_loop(4, 8, turn, 0)
    for k in range(2):
        arrived(k, 2, 0, 0, 2)
        arrived(k, 2, 0, 1, 3)
        along(k, 2)
        across(k, 0)

    for o in range(1, REACH + 1):

        @pl.when(row + o < n_row)
        def _(o=o):
            window(o, row).wait_recv()

    hist[SLOTS] = jnp.zeros((K, NRHS), F32)

    def rows(i, _):
        row_terms(i, table, near, mats, hist)
        return 0

    steps = HALF // UNROLL
    lax.fori_loop(0, steps // 2, rows, 0)
    for k in range(2):
        across(k, -1)
        across(k, 1)
    lax.fori_loop(steps // 2, steps, rows, 0)
    for k in range(2):
        across(k, 2)

    def first(k, d, peer):
        return (
            send(send1.at[k, d], got1.at[k, d], s1_send.at[k, d, 0], s1_recv.at[k, d, 0], {"col": peer}),
            send(step1.at[k, d], gstep1.at[k, d], s1_send.at[k, d, 1], s1_recv.at[k, d, 1], {"col": peer}),
        )

    for d in (1, 0, 2):
        for k in range(2):
            a = shift(at[k], d + 1)

            def code(i, _, k=k, d=d, a=a):
                base = place(k, a, i) * ELEM + k * QUART
                for u in range(QUART):
                    codes, step = coded(total(table, T_LAST_ROW, GROUP, base + u, hist))
                    send1[k, d, i, u] = codes
                    step1[k, d, i, pl.ds(u, 1)] = step
                return 0

            lax.fori_loop(0, SIDE, code, 0)
            for c in first(k, d, place(k, a, at[1 - k])):
                c.start()
    for k in range(2):

        def keep(i, _, k=k):
            base = place(k, at[k], i) * ELEM + k * QUART
            for u in range(QUART):
                own[k, i, u] = total(table, T_LAST_ROW, GROUP, base + u, hist)
            return 0

        lax.fori_loop(0, SIDE, keep, 0)

    for k in range(2):
        for da in (0, -1, 1, 2):
            last(k, da)

    def cols(i, _):
        col_terms(i, table, group, mats, hist)
        return 0

    lax.fori_loop(0, steps, cols, 0)

    def column(o, peer):
        return (
            send(sendc.at[o - 1], gotc.at[o - 1], c_send.at[o - 1, 0], c_recv.at[o - 1, 0], {"row": peer}),
            send(stepc.at[o - 1], gstepc.at[o - 1], c_send.at[o - 1, 1], c_recv.at[o - 1, 1], {"row": peer}),
        )

    for o in range(1, REACH + 1):
        for u in range(ELEM):
            codes, step = coded(total(table, T_LAST_COL, WINDOW, o * ELEM + u, hist))
            sendc[o - 1, u] = codes
            stepc[o - 1, pl.ds(u, 1)] = step

        @pl.when(row + o < n_row)
        def _(o=o):
            for c in column(o, row + o):
                c.start()

    for u in range(ELEM):
        mine[u] = total(table, T_LAST_COL, WINDOW, u, hist)

    def second(k, d, peer):
        return (
            send(send2.at[k, d], got2.at[k, d], s2_send.at[k, d, 0], s2_recv.at[k, d, 0], {"col": peer}),
            send(step2.at[k, d], gstep2.at[k, d], s2_send.at[k, d, 1], s2_recv.at[k, d, 1], {"col": peer}),
        )

    def gathered(k, b, u):
        v = own[k, b, u]
        for d in range(SIDE - 1):
            v = v + decoded(got1[k, d, b, u], gstep1[k, d, b, pl.ds(u, 1)])
        return v

    for k in range(2):
        for d in range(SIDE - 1):
            for c in first(k, d, col):
                c.wait_recv()
        for d in (1, 0, 2):
            b = shift(at[1 - k], d + 1)
            for u in range(QUART):
                codes, step = coded(gathered(k, b, u))
                send2[k, d, u] = codes
                step2[k, d, pl.ds(u, 1)] = step
            for c in second(k, d, place(k, at[k], b)):
                c.start()
    for k in range(2):
        for u in range(QUART):
            mine[k * QUART + u] += gathered(k, at[1 - k], u)

    for o in range(1, REACH + 1):

        @pl.when(row - o >= 0)
        def _(o=o):
            for c in column(o, row):
                c.wait_recv()

    for u in range(ELEM):
        v = mine[u]
        for o in range(REACH):
            v = v + decoded(gotc[o, u], gstepc[o, pl.ds(u, 1)])
        mine[u] = v
    for k in range(2):
        for d in range(SIDE - 1):
            for c in second(k, d, col):
                c.wait_recv()
        for u in range(QUART):
            v = mine[k * QUART + u]
            for d in range(SIDE - 1):
                v = v + decoded(got2[k, d, u], gstep2[k, d, pl.ds(u, 1)])
            out[k * QUART + u] = v

    for c in started:
        c.wait_send()
    for k in range(2):
        for d in range(SIDE - 1):
            for c in (*first(k, d, col), *second(k, d, col)):
                c.wait_send()
    for o in range(1, REACH + 1):

        @pl.when(row - o >= 0)
        def _(o=o):
            window(o, row).wait_send()

        @pl.when(row + o < n_row)
        def _(o=o):
            for c in column(o, row):
                c.wait_send()


def chains(keys, size):
    slots = jnp.arange(SLOTS, dtype=I32)
    before = (slots[None, :] < slots[:, None]) & (slots[None, :] // HALF == slots[:, None] // HALF)
    same = (keys[None, :] == keys[:, None]) & before
    prev = jnp.max(jnp.where(same, slots[None, :], -1), axis=1)
    names = jnp.arange(size, dtype=I32)
    halves = jnp.arange(2, dtype=I32)
    here = (keys[None, None, :] == names[None, :, None]) & (slots[None, None, :] // HALF == halves[:, None, None])
    last = jnp.max(jnp.where(here, slots[None, None, :], -1), axis=2).reshape(-1)
    return jnp.where(prev < 0, SLOTS, prev), jnp.where(last < 0, SLOTS, last)


def body(coeffs, blocks, blk_rows, blk_cols, blk_count):
    my_row = lax.axis_index("row")
    slots = jnp.arange(SLOTS, dtype=I32)
    active = slots < blk_count[0]
    mirror = active & (blk_rows != blk_cols)
    row_local = jnp.clip(blk_rows - my_row * GROUP, 0, GROUP - 1)
    col_local = (blk_cols // GROUP - my_row) * ELEM + blk_cols % ELEM
    col_local = jnp.clip(col_local, 0, WINDOW - 1)
    prev_row, last_row = chains(jnp.where(active, row_local, -1), GROUP)
    prev_col, last_col = chains(jnp.where(mirror, col_local, -1), WINDOW)
    table = jnp.concatenate([col_local, row_local, prev_row, prev_col, last_row, last_col])
    flat = jnp.transpose(blocks, (1, 2, 0)).reshape(K * K, SLOTS)
    side = SIDE - 1
    vmem, dma = pltpu.VMEM, pltpu.SemaphoreType.DMA
    return pl.pallas_call(
        kernel,
        out_shape=jax.ShapeDtypeStruct((ELEM, K, NRHS), F32),
        in_specs=[
            pl.BlockSpec(memory_space=pltpu.SMEM),
            pl.BlockSpec(memory_space=pltpu.VMEM),
            pl.BlockSpec(memory_space=pl.ANY),
        ],
        out_specs=pl.BlockSpec(memory_space=pltpu.VMEM),
        scratch_shapes=[
            vmem((K * K, SLOTS), BF16),
            vmem((HALF * K, 2 * K), F32),
            vmem((SLOTS + 1, K, NRHS), F32),
            vmem((GROUP, K, NRHS), BF16),
            vmem((WINDOW, K, NRHS), BF16),
            vmem((2, SIDE, QUART, K, NRHS), F32),
            vmem((ELEM, K, NRHS), F32),
            vmem((2, side, SIDE, QUART, K, NRHS), I16),
            vmem((2, side, SIDE, ELEM, NRHS), F32),
            vmem((2, side, SIDE, QUART, K, NRHS), I16),
            vmem((2, side, SIDE, ELEM, NRHS), F32),
            vmem((2, side, QUART, K, NRHS), I16),
            vmem((2, side, ELEM, NRHS), F32),
            vmem((2, side, QUART, K, NRHS), I16),
            vmem((2, side, ELEM, NRHS), F32),
            vmem((REACH, ELEM, K, NRHS), I16),
            vmem((REACH, ELEM, NRHS), F32),
            vmem((REACH, ELEM, K, NRHS), I16),
            vmem((REACH, ELEM, NRHS), F32),
            dma((4,)),
            dma((2, 20)),
            dma((2, 20)),
            dma((REACH,)),
            dma((REACH,)),
            dma((2, side, 2)),
            dma((2, side, 2)),
            dma((2, side, 2)),
            dma((2, side, 2)),
            dma((REACH, 2)),
            dma((REACH, 2)),
        ],
        compiler_params=pltpu.CompilerParams(
            collective_id=0, has_side_effects=True, vmem_limit_bytes=56 * 2**20
        ),
        name="near_field",
    )(table, coeffs, flat)


def solution(mesh):
    placed = (
        P(("row", "col"), None, None),
        P(("row", "col"), None, None),
        P(("row", "col")),
        P(("row", "col")),
        P(("row", "col")),
    )
    return jax.shard_map(
        body, mesh=mesh, in_specs=placed, out_specs=P(("row", "col"), None, None), check_vma=False
    )
```

time: 233 us -> 56.3 us (0.24)
  the two profiles are of different devices: /device:TPU:1 before, /device:TPU:96 now
where the time goes in v1:
time: 56.3 us; the launch traced here: 56 us
  Pallas kernels  50.5 us (90%)
  other arithmetic  2.46 us (4%)
  local copies, waits for them, and re-layouts  2.35 us (4%)
  between operations  0.73 us (1%)
    pallas_call x1, Pallas kernels, body(): pl.pallas_call(kernel, out_shape=jax.ShapeDtypeStruct((ELEM, K, NRHS), F3...  50.5 us
    unnamed x3, local copies, waits for them, and re-layouts  2.27 us

profile of v1, /device:TPU:96, one launch (start us, length us, event | category | flops | bytes accessed | tf_op | source)
XLA Modules:
  0.0 56.0 jit_solution(7668019020384637770)
XLA Ops:
  0.7 0.7 %constant_dynamic-update-slice_fusion.5 = s32[2368]{0:T(1024)S(1)} fusion(s32[2368]{0:T(1024)S(1)} %custom-call, s32[]{:T(128)S(6)} %axis_index.15, s32[512]{0:T(512)} %param.8), kind=kLoop, calls=%fused_computation.15 | loop fusion | flops 13824 | bytes 4100
  1.4 0.7 %fusion.9 = (s32[512]{0:T(512)S(1)}, s32[2368]{0:T(1024)S(1)}, s32[512]{0:T(512)S(1)}, s32[512]{0:T(512)S(1)}) fusion(s32[512]{0:T(512)} %param.7, s32[]{:T(128)} %bitcast.6, s32[]{:T(128)S(6)} %mul.11, s32[2368]{0:T(1024)S(1)} %constant_dynamic-update-slice_fusion.5, s32[]{:T(128)S(6)} %axis_index.15, s32[512]{0:T(512)} %param.8), kind=kLoop, calls=%fused_computation.38 | loop fusion | flops 21504 | bytes 12300 | tf_op jit(solution)/shard_map/jit(_where)/select_n | solution.py:393
  2.1 0.7 %select_reduce_fusion = (s32[512]{0:T(512)S(1)}, s32[512]{0:T(512)S(1)}) fusion(s32[512]{0:T(512)S(1)} %get-tuple-element.9, s32[512]{0:T(512)S(1)} %get-tuple-element.10, s32[512]{0:T(512)S(1)} %get-tuple-element.7), kind=kLoop, calls=%fused_computation | loop fusion | flops 2882560 | bytes 10240 | tf_op jit(solution)/shard_map/reduce_max | solution.py:377
  2.8 0.1 select_reduce_fusion.3
  2.9 0.1 reshape.197
  3.1 0.2 select_reduce_fusion.2
  3.3 0.0 copy-start
  3.3 0.6 %copy-done = s32[2368]{0:T(1024)} copy-done((s32[2368]{0:T(1024)}, s32[2368]{0:T(1024)S(1)}, u32[]{:S(2)}) %copy-start) | copy-done | bytes 9496
  3.9 50.5 %near_field.1 = f32[8,64,128]{2,1,0:T(8,128)} custom-call(s32[2368]{0:T(1024)} %copy-done, bf16[8,64,128]{2,1,0:T(8,128)(2,1)} %coeffs.1, bf16[4096,512]{1,0:T(8,128)(2,1)} %bitcast.7), custom_call_target="tpu_custom_call" | custom-call | tf_op jit(solution)/shard_map/near_field/pallas_call | solution.py:399
  54.4 1.7 %copy.14 = f32[8,64,128]{2,1,0:T(8,128)} copy(f32[8,64,128]{2,1,0:T(8,128)} %near_field.1) | data formatting | bytes 524288
  (8 shorter events, 0.1 us)
Async XLA Ops:
  3.3 0.6 %copy-start = (s32[2368]{0:T(1024)}, s32[2368]{0:T(1024)S(1)}, u32[]{:S(2)}) copy-start(s32[2368]{0:T(1024)S(1)} %constant_dynamic-update-slice_fusion.table) | copy-start | bytes 28420

commit v2 on v0

v2 whole, which is shorter than its diff:
```python
import jax
import jax.numpy as jnp
from jax import lax
from jax.experimental import pallas as pl
from jax.experimental.pallas import tpu as pltpu
from jax.sharding import PartitionSpec as P

MESH = pl.DeviceIdType.MESH
F32, BF16, I16, I32 = jnp.float32, jnp.bfloat16, jnp.int16, jnp.int32

K = 64
NRHS = 128
ELEM = 8
SLOTS = 512
HALF = SLOTS // 2
REACH = 3
SIDE = 4
COLS = SIDE * SIDE
GROUP = ELEM * COLS
WINDOW = ELEM * (REACH + 1)
QUART = ELEM // 2
UNROLL = 16
STEP = 32767.0
EXTRA = 16

LANES = 128
TILES = SLOTS // LANES
T_COL, T_ROW, T_PREV_ROW, T_PREV_COL = 0, TILES, 2 * TILES, 3 * TILES
T_LAST_ROW, T_LAST_COL = 4 * TILES, 4 * TILES + 2
T_ROWS = 4 * TILES + 8


def nn(a, b):
    return lax.dot_general(a, b, (((1,), (0,)), ((), ())), preferred_element_type=F32)


def nt(a, b):
    return lax.dot_general(a, b, (((1,), (1,)), ((), ())), preferred_element_type=F32)


def entry(table, name, i, u, half):
    per = LANES // UNROLL
    return table[name + half * (TILES // 2) + lax.div(i, per), lax.rem(i, per) * UNROLL + u]


def add_terms(i, terms, table, prev, hist):
    for u, pair in enumerate(terms):
        for half, term in enumerate(pair):
            hist[half * HALF + i * UNROLL + u] = term + hist[entry(table, prev, i, u, half)]


def row_terms(i, table, near, mats, hist):
    zero = jnp.zeros((K, NRHS), BF16)
    terms = []
    for u in range(UNROLL):
        one, two = (near[entry(table, T_COL, i, u, half)] for half in range(2))
        pair = mats[pl.ds(pl.multiple_of((i * UNROLL + u) * K, K), K), :].astype(BF16)
        both = jnp.concatenate(
            [jnp.concatenate([one, zero], 1), jnp.concatenate([zero, two], 1)], 0
        )
        t = nn(pair, both)
        terms.append((t[:, :NRHS], t[:, NRHS:]))
    add_terms(i, terms, table, T_PREV_ROW, hist)


def col_terms(i, table, group, mats, hist):
    terms = []
    for u in range(UNROLL):
        one, two = (group[entry(table, T_ROW, i, u, half)] for half in range(2))
        pair = mats[pl.ds(pl.multiple_of((i * UNROLL + u) * K, K), K), :].T.astype(BF16)
        terms.append((nn(pair[:K], one), nn(pair[K:], two)))
    add_terms(i, terms, table, T_PREV_COL, hist)


def total(table, name, e, hist):
    return hist[table[name, e]] + hist[table[name + 1, e]]


def tables(count_ref, rows_ref, cols_ref, out):
    rows, cols, count = rows_ref[...], cols_ref[...], count_ref[0]
    my_row = lax.axis_index("row")
    slot = lax.broadcasted_iota(I32, (TILES, LANES), 0) * LANES + lax.broadcasted_iota(I32, (TILES, LANES), 1)
    active = slot < count
    mirror = active & (rows != cols)
    row_local = jnp.clip(rows - my_row * GROUP, 0, GROUP - 1)
    col_local = (lax.shift_right_logical(cols, 7) - my_row) * ELEM + (cols & (ELEM - 1))
    col_local = jnp.clip(col_local, 0, WINDOW - 1)
    out[pl.ds(T_COL, TILES)] = col_local
    out[pl.ds(T_ROW, TILES)] = row_local
    out[pl.ds(T_LAST_COL + 2, T_ROWS - T_LAST_COL - 2)] = jnp.zeros((T_ROWS - T_LAST_COL - 2, LANES), I32)
    down = lax.broadcasted_iota(I32, (LANES, LANES), 0)
    across = lax.broadcasted_iota(I32, (LANES, LANES), 1)
    names = across.astype(F32)
    for key, prev, last in (
        (jnp.where(active, row_local, -1), T_PREV_ROW, T_LAST_ROW),
        (jnp.where(mirror, col_local, -1), T_PREV_COL, T_LAST_COL),
    ):
        key = key.astype(F32)
        wide = [jnp.broadcast_to(key[t : t + 1], (LANES, LANES)) for t in range(TILES)]
        tall = [w.T for w in wide]
        number = [(down + t * LANES).astype(F32) for t in range(TILES)]
        none = jnp.full((LANES, LANES), -1.0, F32)
        for half in range(2):
            low, high = 2 * half, 2 * half + 1
            found = []
            found.append(jnp.where((tall[low] == wide[low]) & (down < across), number[low], none))
            found.append(
                jnp.maximum(
                    jnp.where(tall[low] == wide[high], number[low], none),
                    jnp.where((tall[high] == wide[high]) & (down < across), number[high], none),
                )
            )
            ends = jnp.maximum(
                jnp.where(tall[low] == names, number[low], none),
                jnp.where(tall[high] == names, number[high], none),
            )
            for place, f in ((prev + low, found[0]), (prev + high, found[1]), (last + half, ends)):
                best = jnp.max(f, axis=0, keepdims=True)
                out[pl.ds(place, 1)] = jnp.where(best < 0, float(SLOTS), best).astype(I32)


def coded(values, out):
    n = len(values)
    peaks = [jnp.max(jnp.abs(v), axis=0, keepdims=True) for v in values]
    peaks.append(jnp.ones((EXTRA - n, NRHS), F32))
    power = jnp.ceil(jnp.log2(jnp.maximum(jnp.concatenate(peaks, axis=0), 1e-30)))
    out[pl.ds(n * K, EXTRA)] = power.astype(I32).astype(I16)
    scale = jnp.exp2(-power) * STEP
    for u, v in enumerate(values):
        out[pl.ds(u * K, K)] = jnp.round(v * scale[u : u + 1]).astype(I32).astype(I16)


def decoded(codes, n):
    step = jnp.exp2(codes[pl.ds(n * K, EXTRA)].astype(I32).astype(F32)) * (1.0 / STEP)
    return [codes[pl.ds(u * K, K)].astype(I32).astype(F32) * step[u : u + 1] for u in range(n)]


def kernel(
    table, coeffs, blocks, out, out_cols,
    flat, mats, hist, group, near, own,
    send1, got1, send2, got2, sendc, gotc, swap_out, swap_in, beside_out, beside_in,
    load_sem, ag_send, ag_recv, win_send, win_recv, s1_send, s1_recv, s2_send, s2_recv, c_send, c_recv,
):
    row, col = lax.axis_index("row"), lax.axis_index("col")
    n_row = lax.axis_size("row")
    core = lax.rem(row, 2)
    at = (lax.rem(col, SIDE), lax.div(col, SIDE))

    def place(k, a, b):
        return a * (1 + (SIDE - 1) * k) + b * (SIDE - (SIDE - 1) * k)

    def shift(v, by):
        return lax.rem(v + by + SIDE, SIDE)

    def send(src, dst, s, r, device):
        return pltpu.make_async_remote_copy(
            src_ref=src, dst_ref=dst, send_sem=s, recv_sem=r, device_id=device, device_id_type=MESH
        )

    barrier = pltpu.get_barrier_semaphore()
    for k in range(2):
        for by in range(1, SIDE):
            peer = place(k, shift(at[k], by), at[1 - k])
            pl.semaphore_signal(barrier, inc=1, device_id={"col": peer}, device_id_type=MESH)
    signals = 2 * (SIDE - 1)
    for o in range(1, REACH + 1):
        for r in (row - o, row + o):
            inside = (r >= 0) & (r < n_row)

            @pl.when(inside)
            def _(r=r):
                pl.semaphore_signal(barrier, inc=1, device_id={"row": r}, device_id_type=MESH)

            signals = signals + jnp.where(inside, 1, 0)

    chunk = K * K // 4
    loads = [
        pltpu.make_async_copy(
            blocks.at[pl.ds(i * chunk, chunk)], flat.at[pl.ds(i * chunk, chunk)], load_sem.at[i]
        )
        for i in range(4)
    ]
    for c in loads:
        c.start()
    group[pl.ds(pl.multiple_of(col * ELEM, ELEM), ELEM)] = coeffs[...]
    near[pl.ds(0, ELEM)] = coeffs[...]
    for o in range(1, REACH + 1):

        @pl.when(row + o >= n_row)
        def _(o=o):
            near[pl.ds(o * ELEM, ELEM)] = jnp.zeros((ELEM, K, NRHS), BF16)

    pl.semaphore_wait(barrier, signals)

    def window(o, src, s, peer):
        return send(src, near.at[pl.ds(o * ELEM, ELEM)], win_send.at[s], win_recv.at[o - 1], {"row": peer})

    second_row = near.at[pl.ds(2 * ELEM, ELEM)]
    passed = row + 2 < n_row
    windows = (
        (row >= 2, lambda: window(2, coeffs, 0, row - 2)),
        (core == 1, lambda: window(1, coeffs, 1, row - 1)),
        ((core == 0) & passed & (row >= 2), lambda: window(3, second_row, 1, row - 1)),
        ((core == 0) & passed, lambda: window(1, second_row, 2, row + 1)),
        ((core == 1) & passed, lambda: window(3, second_row, 2, row - 1)),
    )

    def window_arrived(o):
        @pl.when(row + o < n_row)
        def _():
            window(o, coeffs, 0, row).wait_recv()

    for when, make in windows[:2]:

        @pl.when(when)
        def _(make=make):
            make().start()

    def piece(k, da, db, part=None):
        dev = place(k, shift(at[k], da), shift(at[1 - k], db))
        if part is None:
            return group.at[pl.ds(dev * ELEM + k * QUART, QUART)]
        return group.at[pl.ds(dev * ELEM + k * QUART + part * (QUART // 2), QUART // 2)]

    started = []
    order = {0: 0, -1: 1, 1: 2, 2: 3}

    def gather(k, axis, da, db, part, to, index):
        a, b = (shift(at[k], to), at[1 - k]) if axis == 0 else (at[k], shift(at[1 - k], to))
        ref = piece(k, da, db, part)
        c = send(ref, ref, ag_send.at[k, index], ag_recv.at[k, index], {"col": place(k, a, b)})
        c.start()
        started.append(c)

    def arrived(k, da, db, part, index):
        ref = piece(k, da, db, part)
        send(ref, ref, ag_send.at[k, index], ag_recv.at[k, index], {"col": col}).wait_recv()

    def along(k, da):
        gather(k, 1, da, 0, None, 1, 3 + 4 * order[da])
        gather(k, 1, da, 0, None, -1, 4 + 4 * order[da])

    def across(k, da):
        arrived(k, da, -1, None, 3 + 4 * order[da])
        gather(k, 1, da, -1, 0, 1, 5 + 4 * order[da])
        arrived(k, da, 1, None, 4 + 4 * order[da])
        gather(k, 1, da, 1, 1, -1, 6 + 4 * order[da])

    def last(k, da):
        arrived(k, da, 2, 0, 5 + 4 * order[da])
        arrived(k, da, 2, 1, 6 + 4 * order[da])

    for k in range(2):
        gather(k, 0, 0, 0, None, 1, 0)
        gather(k, 0, 0, 0, None, -1, 1)
    for k in range(2):
        gather(k, 0, 0, 0, None, 2, 2)
    for k in range(2):
        along(k, 0)

    r = lax.broadcasted_iota(I32, (HALF, HALF), 0)
    c = lax.broadcasted_iota(I32, (HALF, HALF), 1)
    eye = jnp.where(r == c, 1.0, 0.0).astype(BF16)

    def turn(i, _):
        for u in range(8):
            j = i * 8 + u
            a = flat[pl.ds(pl.multiple_of(j * K, K), K), :]
            a = jnp.concatenate([a[:, :HALF], a[:, HALF:]], axis=0)
            mats[pl.ds(j, HALF, stride=K), :] = nt(eye, a)
        return 0

    for c in loads:
        c.wait()
    lax.fori_loop(0, 8, turn, 0)
    for k in range(2):
        arrived(k, -1, 0, None, 0)
        along(k, -1)
        arrived(k, 1, 0, None, 1)
        along(k, 1)
    window_arrived(2)
    for when, make in windows[2:]:

        @pl.when(when)
        def _(make=make):
            make().start()

    for k in range(2):
        arrived(k, 2, 0, None, 2)
        along(k, 2)
    for k in range(2):
        across(k, 0)
    window_arrived(1)
    window_arrived(3)

    hist[SLOTS] = jnp.zeros((K, NRHS), F32)

    def rows(i, _):
        row_terms(i, table, near, mats, hist)
        return 0

    steps = HALF // UNROLL
    lax.fori_loop(0, steps // 2, rows, 0)
    for k in range(2):
        across(k, -1)
        across(k, 1)
    lax.fori_loop(steps // 2, steps, rows, 0)
    for k in range(2):
        across(k, 2)

    def first(k, d, bo, peer):
        return send(
            send1.at[k, d, bo], got1.at[k, d, bo], s1_send.at[k, d, bo], s1_recv.at[k, d, bo], {"col": peer}
        )

    def pick(k):
        return at[0] * (1 - k) + at[1] * k, at[1] * (1 - k) + at[0] * k

    for bo in (2, 1, 3, 0):

        def code(i, _, bo=bo):
            k, d = lax.rem(i, 2), lax.rem(lax.div(i, 2) + 1, SIDE - 1)
            mine_a, mine_b = pick(k)
            a, b = shift(mine_a, d + 1), shift(mine_b, bo)
            base = place(k, a, b) * ELEM + k * QUART
            coded([total(table, T_LAST_ROW, base + u, hist) for u in range(QUART)], send1.at[k, d, bo])
            first(k, d, bo, place(k, a, mine_b)).start()
            return 0

        lax.fori_loop(0, 2 * (SIDE - 1), code, 0)

    def keep(i, _):
        k, bo = lax.div(i, SIDE), lax.rem(i, SIDE)
        mine_a, mine_b = pick(k)
        base = place(k, mine_a, shift(mine_b, bo)) * ELEM + k * QUART
        for u in range(QUART):
            own[k, bo, u] = total(table, T_LAST_ROW, base + u, hist)
        return 0

    lax.fori_loop(0, 2 * SIDE, keep, 0)

    for k in range(2):
        for da in (0, -1, 1, 2):
            last(k, da)

    def cols(i, _):
        col_terms(i, table, group, mats, hist)
        return 0

    lax.fori_loop(0, steps, cols, 0)

    def swap(peer):
        return send(swap_out, swap_in, c_send.at[0], c_recv.at[0], {"row": peer})

    def beside(peer):
        return send(beside_out, beside_in, c_send.at[1], c_recv.at[1], {"row": peer})

    def column(i, peer):
        return send(sendc.at[i], gotc.at[i], c_send.at[2 + i], c_recv.at[2 + i], {"row": peer})

    other = row + 1 - 2 * core
    for u in range(ELEM):
        swap_out[u] = total(table, T_LAST_COL, (3 - 2 * core) * ELEM + u, hist)

    @pl.when(passed)
    def _():
        swap(other).start()

    @pl.when((core == 1) & (row + 3 < n_row))
    def _():
        coded([total(table, T_LAST_COL, 3 * ELEM + u, hist) for u in range(ELEM)], sendc.at[1])
        column(1, row + 3).start()

    @pl.when(core == 0)
    def _():
        for u in range(ELEM):
            beside_out[u] = total(table, T_LAST_COL, ELEM + u, hist)
        beside(row + 1).start()

    for u in range(ELEM):
        out_cols[u] = total(table, T_LAST_COL, u, hist)

    @pl.when(passed)
    def _():
        swap(other).wait_recv()
        coded([total(table, T_LAST_COL, 2 * ELEM + u, hist) + swap_in[u] for u in range(ELEM)], sendc.at[0])
        column(0, row + 2).start()

    def second(k, d, peer):
        return send(send2.at[k, d], got2.at[k, d], s2_send.at[k, d], s2_recv.at[k, d], {"col": peer})

    def gathered(k, bo):
        for d in range(SIDE - 1):
            first(k, d, bo, col).wait_recv()
        parts = [decoded(got1.at[k, d, bo], QUART) for d in range(SIDE - 1)]
        return [own[k, bo, u] + parts[0][u] + parts[1][u] + parts[2][u] for u in range(QUART)]

    for bo in (2, 1, 3):
        for k in range(2):
            coded(gathered(k, bo), send2.at[k, bo - 1])
            second(k, bo - 1, place(k, at[k], shift(at[1 - k], bo))).start()
    for k in range(2):
        for u, v in enumerate(gathered(k, 0)):
            out[k * QUART + u] = v

    @pl.when(core == 1)
    def _():
        beside(row).wait_recv()
        for u in range(ELEM):
            out_cols[u] += beside_in[u]

    for i, when in ((1, (core == 0) & (row >= 3)), (0, row >= 2)):

        @pl.when(when)
        def _(i=i):
            column(i, row).wait_recv()
            for u, v in enumerate(decoded(gotc.at[i], ELEM)):
                out_cols[u] += v

    for k in range(2):
        for d in range(SIDE - 1):
            second(k, d, col).wait_recv()
        parts = [decoded(got2.at[k, d], QUART) for d in range(SIDE - 1)]
        for u in range(QUART):
            out[k * QUART + u] += parts[0][u] + parts[1][u] + parts[2][u]

    for c in started:
        c.wait_send()
    for k in range(2):
        for d in range(SIDE - 1):
            for bo in range(SIDE):
                first(k, d, bo, col).wait_send()
            second(k, d, col).wait_send()
    for when, make in windows:

        @pl.when(when)
        def _(make=make):
            make().wait_send()

    @pl.when(passed)
    def _():
        for c in (swap(other), column(0, row)):
            c.wait_send()

    @pl.when((core == 1) & (row + 3 < n_row))
    def _():
        column(1, row).wait_send()

    @pl.when(core == 0)
    def _():
        beside(row).wait_send()


def body(coeffs, blocks, blk_rows, blk_cols, blk_count):
    flat = jnp.transpose(blocks, (1, 2, 0)).reshape(K * K, SLOTS)
    side = SIDE - 1
    vmem, dma = pltpu.VMEM, pltpu.SemaphoreType.DMA
    table = pl.pallas_call(
        tables,
        out_shape=jax.ShapeDtypeStruct((T_ROWS, LANES), I32),
        in_specs=[
            pl.BlockSpec(memory_space=pltpu.SMEM),
            pl.BlockSpec(memory_space=pltpu.VMEM),
            pl.BlockSpec(memory_space=pltpu.VMEM),
        ],
        out_specs=pl.BlockSpec(memory_space=pltpu.VMEM),
        name="tables",
    )(blk_count, blk_rows.reshape(TILES, LANES), blk_cols.reshape(TILES, LANES))
    sums, columns = pl.pallas_call(
        kernel,
        out_shape=(jax.ShapeDtypeStruct((ELEM, K, NRHS), F32),) * 2,
        in_specs=[
            pl.BlockSpec(memory_space=pltpu.SMEM),
            pl.BlockSpec(memory_space=pltpu.VMEM),
            pl.BlockSpec(memory_space=pl.ANY),
        ],
        out_specs=(pl.BlockSpec(memory_space=pltpu.VMEM),) * 2,
        scratch_shapes=[
            vmem((K * K, SLOTS), BF16),
            vmem((HALF * K, 2 * K), F32),
            vmem((SLOTS + 1, K, NRHS), F32),
            vmem((GROUP, K, NRHS), BF16),
            vmem((WINDOW, K, NRHS), BF16),
            vmem((2, SIDE, QUART, K, NRHS), F32),
            *[vmem((2, side, SIDE, QUART * K + EXTRA, NRHS), I16)] * 2,
            *[vmem((2, side, QUART * K + EXTRA, NRHS), I16)] * 2,
            *[vmem((2, ELEM * K + EXTRA, NRHS), I16)] * 2,
            *[vmem((ELEM, K, NRHS), F32)] * 4,
            dma((4,)),
            dma((2, 19)),
            dma((2, 19)),
            dma((REACH,)),
            dma((REACH,)),
            dma((2, side, SIDE)),
            dma((2, side, SIDE)),
            dma((2, side)),
            dma((2, side)),
            dma((4,)),
            dma((4,)),
        ],
        compiler_params=pltpu.CompilerParams(
            collective_id=0, has_side_effects=True, vmem_limit_bytes=52 * 2**20
        ),
        name="near_field",
    )(table, coeffs, flat)
    return sums + columns


def solution(mesh):
    placed = (
        P(("row", "col"), None, None),
        P(("row", "col"), None, None),
        P(("row", "col")),
        P(("row", "col")),
        P(("row", "col")),
    )
    return jax.shard_map(
        body, mesh=mesh, in_specs=placed, out_specs=P(("row", "col"), None, None), check_vma=False
    )
```

time: 233 us -> 49.5 us (0.21)
  matrix products: 73.7 us -> 0 us
  waiting for transfers between devices: 66.3 us -> 0 us
  local copies, waits for them, and re-layouts: 52.4 us -> 1.61 us
  Pallas kernels: 0 us -> 46.3 us
  starting transfers between devices: 22.8 us -> 0 us
  between operations: 14.9 us -> 0.66 us
    dot_general x4 -> x0, matrix products: 73.7 us -> none  [the longest x1 24.6 us: body(): jnp.dot(row_select, row_contributions, precision=high_precision, preferre...]
    unnamed x3 -> x0, waiting for transfers between devices: 60.7 us -> none
    pallas_call x0 -> x2, Pallas kernels: none -> 46.3 us  [the longest x1 44.7 us: body(): pl.pallas_call(kernel, out_shape=(jax.ShapeDtypeStruct((ELEM, K, NRHS), F...]
    gather x2 -> x0, local copies, waits for them, and re-layouts: 34.7 us -> none  [the longest x1 21.2 us: body(): row_entries = row_group[row_local]]
    ppermute x6 -> x0, starting transfers between devices: 22.8 us -> none  [from_behind(): return lax.ppermute(block, axis, route)]
    unnamed x8 -> x4, local copies, waits for them, and re-layouts: 16.9 us -> 1.61 us
    ppermute x6 -> x0, waiting for transfers between devices: 5.6 us -> none  [from_behind(): return lax.ppermute(block, axis, route)]
  transfers between devices with their start and end apart: 8 -> 0, of which waited for: 2 -> 0; matrix products, arithmetic and copies ran while one was open for 55% -> 0% of each run, Pallas kernels for 0% -> 0%
where the time goes in v2:
time: 49.5 us; the launch traced here: 49.3 us
  Pallas kernels  46.3 us (94%)
  local copies, waits for them, and re-layouts  1.61 us (3%)
  other arithmetic  0.73 us (1%)
  between operations  0.66 us (1%)
    pallas_call x1, Pallas kernels, body(): pl.pallas_call(kernel, out_shape=(jax.ShapeDtypeStruct((ELEM, K, NRHS), F...  44.7 us
    unnamed x4, local copies, waits for them, and re-layouts  1.61 us
    pallas_call x1, Pallas kernels, body(): pl.pallas_call(tables, out_shape=jax.ShapeDtypeStruct((T_ROWS, LANES), I3...  1.53 us

profile of v2, /device:TPU:1, one launch (start us, length us, event | category | flops | bytes accessed | tf_op | source)
XLA Modules:
  0.0 49.3 jit_solution(15221006196465827116)
XLA Ops:
  0.7 1.5 %tables.1.table = s32[24,128]{1,0:T(8,128)} custom-call(s32[1]{0:T(128)S(6)} %copy.6.count_ref, s32[4,128]{1,0:T(4,128)} %bitcast.6, s32[4,128]{1,0:T(4,128)} %bitcast.7), custom_call_target="tpu_custom_call" | custom-call | tf_op jit(solution)/shard_map/tables/pallas_call | solution.py:458
  2.2 0.0 copy-start
  2.2 0.9 %copy-done = bf16[8,64,128]{2,1,0:T(8,128)(2,1)S(1)} copy-done((bf16[8,64,128]{2,1,0:T(8,128)(2,1)S(1)}, bf16[8,64,128]{2,1,0:T(8,128)(2,1)}, u32[]{:S(2)}) %copy-start) | copy-done | bytes 131096
  3.1 0.0 copy-start.1
  3.1 0.7 %copy-done.1 = s32[24,128]{1,0:T(8,128)S(1)} copy-done((s32[24,128]{1,0:T(8,128)S(1)}, s32[24,128]{1,0:T(8,128)}, u32[]{:S(2)}) %copy-start.1) | copy-done | bytes 12312
  3.8 44.7 %near_field.1 = (f32[8,64,128]{2,1,0:T(8,128)S(1)}, f32[8,64,128]{2,1,0:T(8,128)S(1)}) custom-call(s32[24,128]{1,0:T(8,128)S(1)} %copy-done.1, bf16[8,64,128]{2,1,0:T(8,128)(2,1)S(1)} %copy-done, bf16[4096,512]{1,0:T(8,128)(2,1)} %bitcast.5), custom_call_target="tpu_custom_call" | custom-call | tf_op jit(solution)/shard_map/near_field/pallas_call | solution.py:469
  48.5 0.7 %add.3 = f32[8,64,128]{2,1,0:T(8,128)} add(f32[8,64,128]{2,1,0:T(8,128)S(1)} %get-tuple-element.7, f32[8,64,128]{2,1,0:T(8,128)S(1)} %get-tuple-element.8) | non-fusion elementwise | flops 65536 | bytes 786432 | tf_op jit(solution)/shard_map/add | solution.py:506
Async XLA Ops:
  2.2 0.9 %copy-start = (bf16[8,64,128]{2,1,0:T(8,128)(2,1)S(1)}, bf16[8,64,128]{2,1,0:T(8,128)(2,1)}, u32[]{:S(2)}) copy-start(bf16[8,64,128]{2,1,0:T(8,128)(2,1)} %coeffs.1) | copy-start | bytes 393220
  3.1 0.7 %copy-start.1 = (s32[24,128]{1,0:T(8,128)S(1)}, s32[24,128]{1,0:T(8,128)}, u32[]{:S(2)}) copy-start(s32[24,128]{1,0:T(8,128)} %tables.1.table) | copy-start | bytes 36868

commit v3 on v2

--- a/solution.py
+++ b/solution.py
@@ -182,8 +182,12 @@
     ]
     for c in loads:
         c.start()
-    group[pl.ds(pl.multiple_of(col * ELEM, ELEM), ELEM)] = coeffs[...]
-    near[pl.ds(0, ELEM)] = coeffs[...]
+    loads += [
+        pltpu.make_async_copy(coeffs, group.at[pl.ds(col * ELEM, ELEM)], load_sem.at[4]),
+        pltpu.make_async_copy(coeffs, near.at[pl.ds(0, ELEM)], load_sem.at[5]),
+    ]
+    for c in loads[4:]:
+        c.start()
     for o in range(1, REACH + 1):
 
         @pl.when(row + o >= n_row)
@@ -228,7 +232,8 @@
     def gather(k, axis, da, db, part, to, index):
         a, b = (shift(at[k], to), at[1 - k]) if axis == 0 else (at[k], shift(at[1 - k], to))
         ref = piece(k, da, db, part)
-        c = send(ref, ref, ag_send.at[k, index], ag_recv.at[k, index], {"col": place(k, a, b)})
+        src = coeffs.at[pl.ds(k * QUART, QUART)] if da == 0 and db == 0 else ref
+        c = send(src, ref, ag_send.at[k, index], ag_recv.at[k, index], {"col": place(k, a, b)})
         c.start()
         started.append(c)
 
@@ -300,13 +305,14 @@
         return 0
 
     steps = HALF // UNROLL
-    lax.fori_loop(0, steps // 2, rows, 0)
+    lax.fori_loop(0, steps // 4, rows, 0)
     for k in range(2):
         across(k, -1)
         across(k, 1)
+    lax.fori_loop(steps // 4, steps // 2, rows, 0)
+    for k in range(2):
+        across(k, 2)
     lax.fori_loop(steps // 2, steps, rows, 0)
-    for k in range(2):
-        across(k, 2)
 
     def first(k, d, bo, peer):
         return send(
@@ -471,8 +477,8 @@
         out_shape=(jax.ShapeDtypeStruct((ELEM, K, NRHS), F32),) * 2,
         in_specs=[
             pl.BlockSpec(memory_space=pltpu.SMEM),
-            pl.BlockSpec(memory_space=pltpu.VMEM),
-            pl.BlockSpec(memory_space=pl.ANY),
+            pl.BlockSpec(memory_space=pltpu.HBM),
+            pl.BlockSpec(memory_space=pltpu.HBM),
         ],
         out_specs=(pl.BlockSpec(memory_space=pltpu.VMEM),) * 2,
         scratch_shapes=[
@@ -486,7 +492,7 @@
             *[vmem((2, side, QUART * K + EXTRA, NRHS), I16)] * 2,
             *[vmem((2, ELEM * K + EXTRA, NRHS), I16)] * 2,
             *[vmem((ELEM, K, NRHS), F32)] * 4,
-            dma((4,)),
+            dma((6,)),
             dma((2, 19)),
             dma((2, 19)),
             dma((REACH,)),
@@ -499,7 +505,7 @@
             dma((4,)),
         ],
         compiler_params=pltpu.CompilerParams(
-            collective_id=0, has_side_effects=True, vmem_limit_bytes=52 * 2**20
+            collective_id=0, has_side_effects=True, vmem_limit_bytes=54 * 2**20
         ),
         name="near_field",
     )(table, coeffs, flat)

time: 49.5 us -> 50.2 us (1.014)
  local copies, waits for them, and re-layouts: 1.61 us -> 0 us
  other arithmetic: 0.73 us -> 1.76 us
  Pallas kernels: 46.3 us -> 47.2 us
    unnamed x4 -> x0, local copies, waits for them, and re-layouts: 1.61 us -> none
    add x1, other arithmetic: 0.73 us -> 1.76 us  [body(): return sums + columns]
    pallas_call x1, Pallas kernels: 44.7 us -> 45.7 us  [body(): pl.pallas_call(kernel, out_shape=(jax.ShapeDtypeStruct((ELEM, K, NRHS), F...]
where the time goes in v3:
time: 50.2 us; the launch traced here: 49.6 us
  Pallas kernels  47.2 us (94%)
  other arithmetic  1.76 us (4%)
  between operations  0.66 us (1%)
    pallas_call x1, Pallas kernels, body(): pl.pallas_call(kernel, out_shape=(jax.ShapeDtypeStruct((ELEM, K, NRHS), F...  45.7 us
    add x1, other arithmetic, body(): return sums + columns  1.76 us
    pallas_call x1, Pallas kernels, body(): pl.pallas_call(tables, out_shape=jax.ShapeDtypeStruct((T_ROWS, LANES), I3...  1.53 us

profile of v3, /device:TPU:1, one launch (start us, length us, event | category | flops | bytes accessed | tf_op | source)
XLA Modules:
  0.0 49.6 jit_solution(6944908484841362682)
XLA Ops:
  0.7 1.5 %tables.1.table = s32[24,128]{1,0:T(8,128)} custom-call(s32[1]{0:T(128)S(6)} %copy.6.count_ref, s32[4,128]{1,0:T(4,128)} %bitcast.6, s32[4,128]{1,0:T(4,128)} %bitcast.7), custom_call_target="tpu_custom_call" | custom-call | tf_op jit(solution)/shard_map/tables/pallas_call | solution.py:464
  2.2 45.7 %near_field.1 = (f32[8,64,128]{2,1,0:T(8,128)}, f32[8,64,128]{2,1,0:T(8,128)}) custom-call(s32[24,128]{1,0:T(8,128)} %tables.1.table, bf16[8,64,128]{2,1,0:T(8,128)(2,1)} %coeffs.1, bf16[4096,512]{1,0:T(8,128)(2,1)} %bitcast.5), custom_call_target="tpu_custom_call" | custom-call | tf_op jit(solution)/shard_map/near_field/pallas_call | solution.py:475
  47.9 1.8 %add.3 = f32[8,64,128]{2,1,0:T(8,128)} add(f32[8,64,128]{2,1,0:T(8,128)} %get-tuple-element.7, f32[8,64,128]{2,1,0:T(8,128)} %get-tuple-element.8) | non-fusion elementwise | flops 65536 | bytes 786432 | tf_op jit(solution)/shard_map/add | solution.py:512
